TPU v7x, 768 devices: a whole 4x8x12 slice. The times are simulated.
768 devices in a mesh: dp: 32 (over y, z_hi), tensor: 24 (over x, z_lo, core).
Axes of the slice: x: 4, y: 8, z: 12 (z_hi: 4, z_lo: 3; z = z_hi * 3 + z_lo), core: 2. Of those that a mesh axis runs over, the one named last changes fastest.
Arguments:
- queries: bfloat16 [12288, 3072], P('dp', 'tensor'), may hold values from -6 to 6
- targets: bfloat16 [12288, 3072], P('dp', 'tensor'), may hold values from -6 to 6
- row_lse: float32 [12288], P('dp'), may hold values from 6 to 9
- col_lse: float32 [12288], P('dp'), may hold values from 6 to 9
- positive: int32 [12288], P('dp'), may hold values from 0 to 12287, each once
- target_grads: float32 [12288, 3072], P('dp', 'tensor'), may hold values from -0.75 to 0.75
Outputs:
- query_grads: float32 [12288, 3072], P('dp', 'tensor')
- passed_grads: float32 [12288, 3072], P('dp', 'tensor')
Inputs may be any that keep to these rules, and one draw needn't show every extreme that they name: `positive`: a permutation of the pair indices.
All inputs are finite; a program needn't handle non-finite values.
Results may differ from a plain program's by a relative error of at most 0.0031.
Values may be sent and summed in bfloat16 or wider, within the bound.
A program may use at most 32 MiB of HBM per device.

v0:
```python
import math

import jax
import jax.numpy as jnp
from jax import lax
from jax.sharding import PartitionSpec as P

D = 3072
STEPS = 4


def passed_along(block, axis, distance):
    devices = range(lax.axis_size(axis))
    route = [((i - distance) % len(devices), i) for i in devices]
    return lax.ppermute(block, axis, route)


def weight_block(scores, lse_rows, lse_cols, pos_rows, first_col):
    columns = first_col + jnp.arange(lse_cols.shape[0], dtype=jnp.int32)
    match = (pos_rows[:, None] == columns[None, :]).astype(jnp.float32)
    total = jnp.exp(scores - lse_rows[:, None]) + jnp.exp(scores - lse_cols[None, :]) - 2.0 * match
    return total.astype(jnp.bfloat16)


def shards(queries, targets, row_lse, col_lse, positive, target_grads):
    rows = queries.shape[0]
    scale = 2.0 / math.sqrt(D)
    cycle_size = lax.axis_size("dp")
    place = lax.axis_index("dp")
    current = targets
    accum = target_grads
    lse_cols = col_lse
    grad_q = jnp.zeros(queries.shape, jnp.float32)
    for step in range(STEPS):
        first_col = (place - step) % cycle_size * rows
        partial_scores = lax.dot_general(
            queries, current, (((1,), (1,)), ((), ())), preferred_element_type=jnp.float32
        )
        scores = lax.psum(partial_scores, "tensor") * scale
        weights = weight_block(scores, row_lse, lse_cols, positive, first_col)
        grad_q = grad_q + scale * jnp.dot(weights, current, preferred_element_type=jnp.float32)
        accum = accum + scale * lax.dot_general(
            weights, queries, (((0,), (0,)), ((), ())), preferred_element_type=jnp.float32
        )
        if step + 1 < STEPS:
            current = passed_along(current, "dp", 1)
            accum, lse_cols = passed_along((accum, lse_cols), "dp", 1)
    return (grad_q, accum)


def solution(mesh):
    placed = (P("dp", "tensor"), P("dp", "tensor"), P("dp"), P("dp"), P("dp"), P("dp", "tensor"))
    return jax.shard_map(
        shards,
        mesh=mesh,
        in_specs=placed,
        out_specs=(P("dp", "tensor"), P("dp", "tensor")),
        check_vma=False,
    )
```

profile of v0, /device:TPU:1, one launch (start us, length us, event | category | flops | bytes accessed | tf_op | source)
XLA Modules:
  0.0 355.5 jit_solution(13151712171147448272)
XLA Ops:
  7.2 0.0 copy-start
  7.2 0.0 all-reduce.3.cloned.1.call-start
  7.2 8.4 %collective-permute-start = (bf16[384,128]{1,0:T(8,128)(2,1)}, bf16[384,128]{1,0:T(8,128)(2,1)S(1)}, u32[]{:S(2)}, u32[]{:S(2)}) collective-permute-start(bf16[384,128]{1,0:T(8,128)(2,1)} %param.7), channel_id=1, source_target_pairs={{744,0},{0,24},{24,48},{48,72},{72,96},{96,120},{120,144},{144,168... | collective-permute-start | bytes 294920 | tf_op jit(solution)/shard_map/ppermute | solution.py:15
  15.7 0.0 copy-done
  15.7 2.0 fusion.5
  17.7 9.9 %collective-permute-done = bf16[384,128]{1,0:T(8,128)(2,1)S(1)} collective-permute-done((bf16[384,128]{1,0:T(8,128)(2,1)}, bf16[384,128]{1,0:T(8,128)(2,1)S(1)}, u32[]{:S(2)}, u32[]{:S(2)}) %collective-permute-start) | collective-permute-done | bytes 98336 | tf_op jit(solution)/shard_map/ppermute | solution.py:15
  27.7 1.9 collective-permute-start.2
  29.6 1.1 fusion.7
  30.7 11.3 %collective-permute-done.2 = bf16[384,128]{1,0:T(8,128)(2,1)S(1)} collective-permute-done((bf16[384,128]{1,0:T(8,128)(2,1)S(1)}, bf16[384,128]{1,0:T(8,128)(2,1)S(1)}, u32[]{:S(2)}, u32[]{:S(2)}) %collective-permute-start.2) | collective-permute-done | bytes 98336 | tf_op jit(solution)/shard_map/ppermute | solution.py:15
  42.0 1.9 collective-permute-start.4
  43.9 1.1 fusion.8
  45.0 11.2 %collective-permute-done.4 = bf16[384,128]{1,0:T(8,128)(2,1)S(1)} collective-permute-done((bf16[384,128]{1,0:T(8,128)(2,1)S(1)}, bf16[384,128]{1,0:T(8,128)(2,1)S(1)}, u32[]{:S(2)}, u32[]{:S(2)}) %collective-permute-start.4) | collective-permute-done | bytes 98336 | tf_op jit(solution)/shard_map/ppermute | solution.py:15
  56.2 1.1 fusion.9
  57.3 0.0 copy-start.3
  57.3 0.0 all-reduce.3.cloned.1.call-update
  57.4 0.7 copy-done.3
  58.0 1.9 collective-permute-start.1
  60.0 7.5 %collective-permute-done.1 = f32[384]{0:T(512)S(1)} collective-permute-done((f32[384]{0:T(512)S(1)}, f32[384]{0:T(512)S(1)}, u32[]{:S(2)}, u32[]{:S(2)}) %collective-permute-start.1) | collective-permute-done | bytes 1568 | tf_op jit(solution)/shard_map/ppermute | solution.py:15
  67.4 1.9 collective-permute-start.3
  69.4 7.5 %collective-permute-done.3 = f32[384]{0:T(512)S(1)} collective-permute-done((f32[384]{0:T(512)S(1)}, f32[384]{0:T(512)S(1)}, u32[]{:S(2)}, u32[]{:S(2)}) %collective-permute-start.3) | collective-permute-done | bytes 1568 | tf_op jit(solution)/shard_map/ppermute | solution.py:15
  76.9 1.9 collective-permute-start.5
  78.8 7.5 %collective-permute-done.5 = f32[384]{0:T(512)S(1)} collective-permute-done((f32[384]{0:T(512)S(1)}, f32[384]{0:T(512)S(1)}, u32[]{:S(2)}, u32[]{:S(2)}) %collective-permute-start.5) | collective-permute-done | bytes 1568 | tf_op jit(solution)/shard_map/ppermute | solution.py:15
  86.3 193.8 %all-reduce.3.cloned.1.call-done = (f32[384,384]{1,0:T(8,128)}, f32[384,384]{1,0:T(8,128)}, f32[384,384]{1,0:T(8,128)}, f32[384,384]{1,0:T(8,128)}) async-done(((f32[384,384]{1,0:T(8,128)}, f32[384,384]{1,0:T(8,128)}, f32[384,384]{1,0:T(8,128)}, f32[384,384]{1,0:T(8,128)}), (f32[384,384]{1,0:T(8,128)}, f32[384,384]{1,0:T(8,128)}, f32[384,384]{1,0:T(8,128)}, ...) | async-done | bytes 2359312 | tf_op jit(solution)/shard_map/psum | solution.py:39
  280.1 0.0 copy-start.5
  280.1 0.0 copy-start.4
  280.1 0.7 copy-done.5
  280.8 0.0 copy-done.4
  280.8 0.0 copy-start.1
  280.8 2.7 subtract_convert_fusion
  283.6 0.0 copy-done.1
  283.6 0.0 copy-start.2
  283.6 0.2 fusion.6
  283.8 0.7 copy-done.2
  284.5 0.3 fusion.1
  284.8 16.4 %collective-permute-start.6 = (f32[384,128]{1,0:T(8,128)S(1)}, f32[384,128]{1,0:T(8,128)S(1)}, u32[]{:S(2)}, u32[]{:S(2)}) collective-permute-start(f32[384,128]{1,0:T(8,128)S(1)} %fusion.1), channel_id=1, source_target_pairs={{744,0},{0,24},{24,48},{48,72},{72,96},{96,120},{120,144},{144,168... | collective-permute-start | bytes 589832 | tf_op jit(solution)/shard_map/ppermute | solution.py:15
  301.2 0.2 convolution_add_fusion.2
  301.4 2.3 collective-permute-done.6
  303.8 0.3 fusion
  304.1 12.9 %collective-permute-start.7 = (f32[384,128]{1,0:T(8,128)S(1)}, f32[384,128]{1,0:T(8,128)S(1)}, u32[]{:S(2)}, u32[]{:S(2)}) collective-permute-start(f32[384,128]{1,0:T(8,128)S(1)} %fusion), channel_id=1, source_target_pairs={{744,0},{0,24},{24,48},{48,72},{72,96},{96,120},{120,144},{144,168... | collective-permute-start | bytes 589832 | tf_op jit(solution)/shard_map/ppermute | solution.py:15
  317.0 0.2 convolution_add_fusion.1
  317.2 18.0 %collective-permute-done.7 = f32[384,128]{1,0:T(8,128)S(1)} collective-permute-done((f32[384,128]{1,0:T(8,128)S(1)}, f32[384,128]{1,0:T(8,128)S(1)}, u32[]{:S(2)}, u32[]{:S(2)}) %collective-permute-start.7) | collective-permute-done | bytes 196640 | tf_op jit(solution)/shard_map/ppermute | solution.py:15
  335.3 0.3 fusion.3
  335.6 1.9 collective-permute-start.8
  337.5 0.9 fusion.2
  338.4 9.2 %collective-permute-done.8 = f32[384,128]{1,0:T(8,128)S(1)} collective-permute-done((f32[384,128]{1,0:T(8,128)S(1)}, f32[384,128]{1,0:T(8,128)S(1)}, u32[]{:S(2)}, u32[]{:S(2)}) %collective-permute-start.8) | collective-permute-done | bytes 196640 | tf_op jit(solution)/shard_map/ppermute | solution.py:15
  347.6 1.0 fusion.4
  (2 shorter events, 0.0 us)
Async XLA Ops:
  7.2 8.5 %copy-start = (bf16[384,128]{1,0:T(8,128)(2,1)S(1)}, bf16[384,128]{1,0:T(8,128)(2,1)}, u32[]{:S(2)}) copy-start(bf16[384,128]{1,0:T(8,128)(2,1)} %param.6) | copy-start | bytes 294916
  7.2 272.9 %all-reduce.3.cloned.1.call-start = ((), (), s32[]{:S(2)}) async-start(), calls=%async_computation | async-start | bytes 4718592 | tf_op jit(solution)/shard_map/psum | solution.py:39
  7.2 20.4 %collective-permute-start = (bf16[384,128]{1,0:T(8,128)(2,1)}, bf16[384,128]{1,0:T(8,128)(2,1)S(1)}, u32[]{:S(2)}, u32[]{:S(2)}) collective-permute-start(bf16[384,128]{1,0:T(8,128)(2,1)} %param.7), channel_id=1, source_target_pairs={{744,0},{0,24},{24,48},{48,72},{72,96},{96,120},{120,144},{144,168... | collective-permute-start | bytes 294920 | tf_op jit(solution)/shard_map/ppermute | solution.py:15
  27.7 14.3 %collective-permute-start.2 = (bf16[384,128]{1,0:T(8,128)(2,1)S(1)}, bf16[384,128]{1,0:T(8,128)(2,1)S(1)}, u32[]{:S(2)}, u32[]{:S(2)}) collective-permute-start(bf16[384,128]{1,0:T(8,128)(2,1)S(1)} %collective-permute-done), channel_id=1, source_target_pairs={{744,0},{0,24},{24,48},{48,72},{72,96},{96,120},{120,144},{144,168... | collective-permute-start | bytes 294920 | tf_op jit(solution)/shard_map/ppermute | solution.py:15
  42.0 14.2 %collective-permute-start.4 = (bf16[384,128]{1,0:T(8,128)(2,1)S(1)}, bf16[384,128]{1,0:T(8,128)(2,1)S(1)}, u32[]{:S(2)}, u32[]{:S(2)}) collective-permute-start(bf16[384,128]{1,0:T(8,128)(2,1)S(1)} %collective-permute-done.2), channel_id=1, source_target_pairs={{744,0},{0,24},{24,48},{48,72},{72,96},{96,120},{120,144},{144,168... | collective-permute-start | bytes 294920 | tf_op jit(solution)/shard_map/ppermute | solution.py:15
  57.3 0.7 copy-start.3
  58.0 9.4 %collective-permute-start.1 = (f32[384]{0:T(512)S(1)}, f32[384]{0:T(512)S(1)}, u32[]{:S(2)}, u32[]{:S(2)}) collective-permute-start(f32[384]{0:T(512)S(1)} %copy-done.3), channel_id=1, source_target_pairs={{744,0},{0,24},{24,48},{48,72},{72,96},{96,120},{120,144},{144,168... | collective-permute-start | bytes 4616 | tf_op jit(solution)/shard_map/ppermute | solution.py:15
  67.4 9.4 %collective-permute-start.3 = (f32[384]{0:T(512)S(1)}, f32[384]{0:T(512)S(1)}, u32[]{:S(2)}, u32[]{:S(2)}) collective-permute-start(f32[384]{0:T(512)S(1)} %collective-permute-done.1), channel_id=1, source_target_pairs={{744,0},{0,24},{24,48},{48,72},{72,96},{96,120},{120,144},{144,168... | collective-permute-start | bytes 4616 | tf_op jit(solution)/shard_map/ppermute | solution.py:15
  76.9 9.5 %collective-permute-start.5 = (f32[384]{0:T(512)S(1)}, f32[384]{0:T(512)S(1)}, u32[]{:S(2)}, u32[]{:S(2)}) collective-permute-start(f32[384]{0:T(512)S(1)} %collective-permute-done.3), channel_id=1, source_target_pairs={{744,0},{0,24},{24,48},{48,72},{72,96},{96,120},{120,144},{144,168... | collective-permute-start | bytes 4616 | tf_op jit(solution)/shard_map/ppermute | solution.py:15
  280.1 0.7 copy-start.5
  280.1 0.7 copy-start.4
  280.8 2.7 copy-start.1
  283.6 0.9 copy-start.2
  284.8 19.0 %collective-permute-start.6 = (f32[384,128]{1,0:T(8,128)S(1)}, f32[384,128]{1,0:T(8,128)S(1)}, u32[]{:S(2)}, u32[]{:S(2)}) collective-permute-start(f32[384,128]{1,0:T(8,128)S(1)} %fusion.1), channel_id=1, source_target_pairs={{744,0},{0,24},{24,48},{48,72},{72,96},{96,120},{120,144},{144,168... | collective-permute-start | bytes 589832 | tf_op jit(solution)/shard_map/ppermute | solution.py:15
  304.1 31.2 %collective-permute-start.7 = (f32[384,128]{1,0:T(8,128)S(1)}, f32[384,128]{1,0:T(8,128)S(1)}, u32[]{:S(2)}, u32[]{:S(2)}) collective-permute-start(f32[384,128]{1,0:T(8,128)S(1)} %fusion), channel_id=1, source_target_pairs={{744,0},{0,24},{24,48},{48,72},{72,96},{96,120},{120,144},{144,168... | collective-permute-start | bytes 589832 | tf_op jit(solution)/shard_map/ppermute | solution.py:15
  335.6 12.1 %collective-permute-start.8 = (f32[384,128]{1,0:T(8,128)S(1)}, f32[384,128]{1,0:T(8,128)S(1)}, u32[]{:S(2)}, u32[]{:S(2)}) collective-permute-start(f32[384,128]{1,0:T(8,128)S(1)} %fusion.3), channel_id=1, source_target_pairs={{744,0},{0,24},{24,48},{48,72},{72,96},{96,120},{120,144},{144,168... | collective-permute-start | bytes 589832 | tf_op jit(solution)/shard_map/ppermute | solution.py:15
Sparse Core Ops, SparseCore 0:
  57.5 222.5 all-reduce.2
where the time goes:
time: 360 us; the launch traced here: 355 us
  waiting for transfers between devices  278 us (77%)
  starting transfers between devices  49.3 us (14%)
  between operations  14.3 us (4%)
  matrix products  8.72 us (2%)
    psum x1, waiting for transfers between devices, shards(): scores = lax.psum(partial_scores, 'tensor') * scale  194 us
    ppermute x9, waiting for transfers between devices, passed_along(): return lax.ppermute(block, axis, route)  84.6 us
    ppermute x9, starting transfers between devices, passed_along(): return lax.ppermute(block, axis, route)  49.2 us
  transfers between devices with their start and end apart: 10, of which 10 were waited for; matrix products, arithmetic and copies ran while one was open for 2% of the time, Pallas kernels for 0%

commit v1 on v0

v1 whole, which is shorter than its diff:
```python
import functools
import math

import jax
import jax.numpy as jnp
from jax import lax
from jax.experimental import pallas as pl
from jax.experimental.pallas import tpu as pltpu
from jax.sharding import PartitionSpec as P

D = 3072
STEPS = 4
NX, NZ, NC = 4, 3, 2
SCALE = 2.0 / math.sqrt(D)
COPIES = 64
F32 = jnp.float32
BF16 = jnp.bfloat16


def kernel(
    n_dp, q_ref, t_ref, rl_ref, cl_ref, pos_ref, tg_ref, gq_ref, gt_ref,
    qp, qo, ta, tb, cls, sp, xr, zs, zr, w, gts, g1, gr1, g2, gr2, send_sem, recv_sem,
):
    rows = q_ref.shape[0]
    band = rows // (NX * NZ * NC)
    xband = band * NZ
    half = rows // 2
    b = lax.axis_index("dp")
    t = lax.axis_index("tensor")
    x, zl, c = t // (NZ * NC), lax.rem(t // NC, NZ), lax.rem(t, NC)

    def at_dp(k):
        return (lax.rem(b + k + n_dp, n_dp), t)

    def at_x(k):
        return (b, lax.rem(x + k, NX) * (NZ * NC) + zl * NC + c)

    def at_z(k):
        return (b, x * (NZ * NC) + lax.rem(zl + k, NZ) * NC + c)

    mate = (b, t + 1 - 2 * c)

    barrier = pltpu.get_barrier_semaphore()
    partners = [mate] + [at_x(k) for k in (1, 2, 3)] + [at_z(k) for k in (1, 2)]
    partners += [at_dp(k) for k in (1, -1, 2, -2, 3, -3)]
    for dev in partners:
        pl.semaphore_signal(barrier, inc=1, device_id=dev, device_id_type=pl.DeviceIdType.MESH)

    for i in range(NX * NZ):
        for p in range(NC):
            qp[p, band * i : band * (i + 1)] = q_ref[band * (NC * i + p) : band * (NC * i + p + 1)]

    pl.semaphore_wait(barrier, len(partners))

    started = []

    def send(src, dst, dev):
        i = len(started)
        copy = pltpu.make_async_remote_copy(
            src_ref=src, dst_ref=dst, send_sem=send_sem.at[i], recv_sem=recv_sem.at[i],
            device_id=dev, device_id_type=pl.DeviceIdType.MESH,
        )
        copy.start()
        started.append(copy)
        return copy

    own = [t_ref, ta.at[0], ta.at[1], ta.at[2]]
    got_q = send(qp.at[1 - c], qo, mate)
    got_tb = [None] * STEPS
    got_tb[0] = send(t_ref, tb.at[0], mate)
    got_t1 = send(t_ref, ta.at[0], at_dp(1))
    got_t3 = send(t_ref, ta.at[2], at_dp(3))
    got_cl = [None] + [send(cl_ref, cls.at[k - 1], at_dp(k)) for k in (1, 2, 3)]

    lane = lax.broadcasted_iota(jnp.int32, (band, rows), 1)
    here = lane == t * band + lax.broadcasted_iota(jnp.int32, (band, rows), 0)
    rl = jnp.sum(jnp.where(here, rl_ref[...], 0.0), axis=1, keepdims=True)
    pos = jnp.sum(jnp.where(here, pos_ref[...], 0), axis=1, keepdims=True)

    got_x, got_z, got_zw, got_xw, got_cw = {}, {}, {}, {}, {}

    def scores(d):
        got_tb[d].wait_recv()
        qq = jnp.concatenate([qp[c], qo[...]], axis=1)
        tt = jnp.concatenate([own[d][...], tb[d]], axis=1)
        s = lax.dot_general(qq, tt, (((1,), (1,)), ((), ())), preferred_element_type=F32)
        sp[d] = s.reshape(NX, xband, rows)
        got_x[d] = [send(sp.at[d, lax.rem(x + k, NX)], xr.at[d, k - 1], at_x(k)) for k in (1, 2, 3)]

    def sum_x(d):
        for copy in got_x[d]:
            copy.wait_recv()
        s = sp[d, x] + xr[d, 0] + xr[d, 1] + xr[d, 2]
        zs[d] = s.reshape(NZ, band, rows)
        got_z[d] = [send(zs.at[d, lax.rem(zl + k, NZ)], zr.at[d, k - 1], at_z(k)) for k in (1, 2)]

    def weigh(d):
        for copy in got_z[d]:
            copy.wait_recv()
        s = (zs[d, zl] + zr[d, 0] + zr[d, 1]) * SCALE
        if d:
            got_cl[d].wait_recv()
        cl = cls[d - 1] if d else cl_ref[...]
        match = (pos == lax.rem(b - d + n_dp, n_dp) * rows + lane).astype(F32)
        band_w = jnp.exp(s - rl) + jnp.exp(s - cl) - 2.0 * match
        mine = pl.ds(pl.multiple_of(zl * band, band), band)
        w[d, c, x, mine] = band_w.astype(BF16)
        got_zw[d] = [send(w.at[d, c, x, mine], w.at[d, c, x, mine], at_z(k)) for k in (1, 2)]

    def gather_x(d):
        for k, copy in enumerate(got_zw[d]):
            copy.wait_recv()
        got_xw[d] = [send(w.at[d, c, x], w.at[d, c, x], at_x(k)) for k in (1, 2, 3)]

    def gather_core(d):
        for copy in got_xw[d]:
            copy.wait_recv()
        got_cw[d] = send(w.at[d, c], w.at[d, c], mate)

    def gradients(d):
        got_cw[d].wait_recv()
        weights = w[d].reshape(rows, rows)
        part = jnp.dot(weights, own[d][...], preferred_element_type=F32) * SCALE
        for p in range(NC):
            for i in range(NX * NZ):
                to = slice(band * (NC * i + p), band * (NC * i + p + 1))
                piece = part[half * p + band * i : half * p + band * (i + 1)]
                gq_ref[to] = piece if d == 1 else gq_ref[to] + piece
        queries = qp[...].reshape(rows, q_ref.shape[1])
        term = lax.dot_general(weights, queries, (((0,), (0,)), ((), ())), preferred_element_type=F32)
        return term * SCALE

    scores_0_ready = got_q
    scores_0_ready.wait_recv()
    scores(0)
    sum_x(0)
    got_t1.wait_recv()
    got_t2a = send(ta.at[0, pl.ds(0, half)], ta.at[1, pl.ds(0, half)], at_dp(1))
    got_tb[1] = send(ta.at[0], tb.at[1], mate)
    got_t3.wait_recv()
    got_t2b = send(ta.at[2, pl.ds(half, half)], ta.at[1, pl.ds(half, half)], at_dp(-1))
    got_tb[3] = send(ta.at[2], tb.at[3], mate)
    scores(1)
    scores(3)
    weigh(0)
    sum_x(1)
    sum_x(3)
    gather_x(0)
    weigh(1)
    weigh(3)
    got_t2a.wait_recv()
    got_t2b.wait_recv()
    got_tb[2] = send(ta.at[1], tb.at[2], mate)
    gather_x(1)
    gather_x(3)
    scores(2)
    gather_core(0)
    sum_x(2)
    gather_core(1)
    gather_core(3)
    weigh(2)
    term = gradients(1)
    g1[...] = term.astype(BF16).reshape(g1.shape)
    got_1a = send(g1.at[0], gr1.at[0], at_dp(1))
    got_1b = send(g1.at[1], gr1.at[1], at_dp(-1))
    gather_x(2)
    gts[0] = gradients(0) + tg_ref[...]
    got_1b.wait_recv()
    g2[0, :half] = gts[0, :half].astype(BF16)
    g2[0, half:] = (gts[0, half:] + gr1[1].astype(F32)).astype(BF16)
    got_20 = send(g2.at[0], gr2.at[0], at_dp(3))
    gts[1] = gradients(3)
    gather_core(2)
    gts[0] = gradients(2)
    got_1a.wait_recv()
    g2[1, :half] = (gts[0, :half] + gr1[0].astype(F32)).astype(BF16)
    g2[1, half:] = gts[0, half:].astype(BF16)
    got_22 = send(g2.at[1], gr2.at[1], at_dp(1))
    got_20.wait_recv()
    got_22.wait_recv()
    gt_ref[...] = gts[1] + (gr2[0].astype(F32) + gr2[1].astype(F32))
    for copy in started:
        copy.wait_send()


def shards(n_dp, queries, targets, row_lse, col_lse, positive, target_grads):
    rows, cols = queries.shape
    band, half = rows // (NX * NZ * NC), rows // 2
    vmem = pl.BlockSpec(memory_space=pltpu.VMEM)
    return pl.pallas_call(
        functools.partial(kernel, n_dp),
        out_shape=(jax.ShapeDtypeStruct((rows, cols), F32),) * 2,
        in_specs=[vmem] * 6,
        out_specs=(vmem, vmem),
        scratch_shapes=[
            pltpu.VMEM((NC, half, cols), BF16),
            pltpu.VMEM((half, cols), BF16),
            pltpu.VMEM((STEPS - 1, rows, cols), BF16),
            pltpu.VMEM((STEPS, rows, cols), BF16),
            pltpu.VMEM((STEPS - 1, 1, rows), F32),
            pltpu.VMEM((STEPS, NX, band * NZ, rows), F32),
            pltpu.VMEM((STEPS, NX - 1, band * NZ, rows), F32),
            pltpu.VMEM((STEPS, NZ, band, rows), F32),
            pltpu.VMEM((STEPS, NZ - 1, band, rows), F32),
            pltpu.VMEM((STEPS, NC, NX, band * NZ, rows), BF16),
            pltpu.VMEM((2, rows, cols), F32),
            pltpu.VMEM((2, half, cols), BF16),
            pltpu.VMEM((2, half, cols), BF16),
            pltpu.VMEM((2, rows, cols), BF16),
            pltpu.VMEM((2, rows, cols), BF16),
            pltpu.SemaphoreType.DMA((COPIES,)),
            pltpu.SemaphoreType.DMA((COPIES,)),
        ],
        compiler_params=pltpu.CompilerParams(
            collective_id=0, has_side_effects=True, vmem_limit_bytes=40 << 20
        ),
        cost_estimate=pl.CostEstimate(flops=10**9, bytes_accessed=10**6, transcendentals=10**5),
    )(
        queries, targets, row_lse.reshape(1, rows), col_lse.reshape(1, rows),
        positive.reshape(1, rows), target_grads,
    )


def solution(mesh):
    placed = (P("dp", "tensor"), P("dp", "tensor"), P("dp"), P("dp"), P("dp"), P("dp", "tensor"))
    return jax.shard_map(
        functools.partial(shards, mesh.shape["dp"]),
        mesh=mesh,
        in_specs=placed,
        out_specs=(P("dp", "tensor"), P("dp", "tensor")),
        check_vma=False,
    )
```

time: 360 us -> 78.3 us (0.22)
  waiting for transfers between devices: 278 us -> 0 us
  Pallas kernels: 0 us -> 71 us
  starting transfers between devices: 49.3 us -> 0 us
  between operations: 14.3 us -> 0.66 us
  matrix products: 8.72 us -> 0 us
    psum x1 -> x0, waiting for transfers between devices: 194 us -> none  [shards(): scores = lax.psum(partial_scores, 'tensor') * scale]
    ppermute x9 -> x0, waiting for transfers between devices: 84.6 us -> none  [passed_along(): return lax.ppermute(block, axis, route)]
    pallas_call x0 -> x1, Pallas kernels: none -> 71 us  [shards(): pl.pallas_call(functools.partial(kernel, n_dp), out_shape=(jax.ShapeDtype...]
    ppermute x9 -> x0, starting transfers between devices: 49.2 us -> none  [passed_along(): return lax.ppermute(block, axis, route)]
    dot_general x12 -> x0, matrix products: 8.72 us -> none  [the longest x4 5.28 us: shards(): lax.dot_general(queries, current, (((1,), (1,)), ((), ())), preferred_ele...]
  transfers between devices with their start and end apart: 10 -> 0, of which waited for: 10 -> 0; matrix products, arithmetic and copies ran while one was open for 2% -> 0% of each run, Pallas kernels for 0% -> 0%
where the time goes in v1:
time: 78.3 us; the launch traced here: 77.1 us
  Pallas kernels  71 us (91%)
  local copies, waits for them, and re-layouts  5.44 us (7%)
    pallas_call x1, Pallas kernels, shards(): pl.pallas_call(functools.partial(kernel, n_dp), out_shape=(jax.ShapeDtype...  71 us
    unnamed x12, local copies, waits for them, and re-layouts  4.75 us

profile of v1, /device:TPU:1, one launch (start us, length us, event | category | flops | bytes accessed | tf_op | source)
XLA Modules:
  0.0 77.1 jit_solution(14573206708956378166)
XLA Ops:
  0.6 0.0 copy-start.3
  0.6 0.7 reshape.13.rl_ref
  1.3 0.0 copy-done.3
  1.3 0.0 copy-start.4
  1.3 0.7 copy-done.4
  2.0 0.0 copy-start
  2.0 0.9 %copy-done = f32[384,128]{1,0:T(8,128)S(1)} copy-done((f32[384,128]{1,0:T(8,128)S(1)}, f32[384,128]{1,0:T(8,128)}, u32[]{:S(2)}) %copy-start) | copy-done | bytes 196632
  2.9 0.0 copy-start.1
  2.9 0.9 %copy-done.1 = bf16[384,128]{1,0:T(8,128)(2,1)S(1)} copy-done((bf16[384,128]{1,0:T(8,128)(2,1)S(1)}, bf16[384,128]{1,0:T(8,128)(2,1)}, u32[]{:S(2)}) %copy-start.1) | copy-done | bytes 98328
  3.8 0.0 copy-start.2
  3.8 0.9 %copy-done.2 = bf16[384,128]{1,0:T(8,128)(2,1)S(1)} copy-done((bf16[384,128]{1,0:T(8,128)(2,1)S(1)}, bf16[384,128]{1,0:T(8,128)(2,1)}, u32[]{:S(2)}) %copy-start.2) | copy-done | bytes 98328
  4.7 71.0 %shard_map.77 = (f32[384,128]{1,0:T(8,128)S(1)}, f32[384,128]{1,0:T(8,128)S(1)}) custom-call(bf16[384,128]{1,0:T(8,128)(2,1)S(1)} %copy-done.1, bf16[384,128]{1,0:T(8,128)(2,1)S(1)} %copy-done.2, f32[1,384]{1,0:T(1,128)S(1)} %reshape.13.rl_ref, f32[1,384]{1,0:T(1,128)S(1)} %reshape.14.cl_ref, s32[1,384]{1,0:T(1,128)S(1)} %reshape.15.pos_ref, ...), custom_call_target="tpu_custom_call" | custom-call | flops 1000000000 | bytes 1000000 | tf_op jit(solution)/shard_map/pallas_call | solution.py:190
  75.7 0.7 copy.10
  76.4 0.7 copy.11
  (2 shorter events, 0.0 us)
Async XLA Ops:
  0.6 0.7 copy-start.3
  1.3 0.7 copy-start.4
  2.0 0.9 %copy-start = (f32[384,128]{1,0:T(8,128)S(1)}, f32[384,128]{1,0:T(8,128)}, u32[]{:S(2)}) copy-start(f32[384,128]{1,0:T(8,128)} %tg_ref.1) | copy-start | bytes 589828
  2.9 0.9 %copy-start.1 = (bf16[384,128]{1,0:T(8,128)(2,1)S(1)}, bf16[384,128]{1,0:T(8,128)(2,1)}, u32[]{:S(2)}) copy-start(bf16[384,128]{1,0:T(8,128)(2,1)} %q_ref.1) | copy-start | bytes 294916
  3.8 0.9 %copy-start.2 = (bf16[384,128]{1,0:T(8,128)(2,1)S(1)}, bf16[384,128]{1,0:T(8,128)(2,1)}, u32[]{:S(2)}) copy-start(bf16[384,128]{1,0:T(8,128)(2,1)} %t_ref.1) | copy-start | bytes 294916

commit v2 on v1

v2 whole, which is shorter than its diff:
```python
import functools
import math

import jax
import jax.numpy as jnp
from jax import lax
from jax.experimental import pallas as pl
from jax.experimental.pallas import tpu as pltpu
from jax.sharding import PartitionSpec as P

D = 3072
STEPS = 4
NX, NZ, NC = 4, 3, 2
SCALE = 2.0 / math.sqrt(D)
COPIES = 80
LOADS = 6
F32 = jnp.float32
BF16 = jnp.bfloat16
I16 = jnp.int16
BOUND = 6.0
LEVELS = 32767.0


def code_of(reach, knee):
    steps = LEVELS / math.asinh(reach / knee)

    def encode(v):
        a = jnp.abs(v) * (1.0 / knee)
        u = jnp.minimum(jnp.log(a + jnp.sqrt(a * a + 1.0)) * steps, LEVELS)
        return jnp.round(jnp.where(v < 0, -u, u)).astype(jnp.int32).astype(I16)

    def decode(q):
        e = jnp.exp(q.astype(jnp.int32).astype(F32) * (1.0 / steps))
        return (e - 1.0 / e) * (0.5 * knee)

    return encode, decode


def kernel(
    n_dp, q_hbm, t_hbm, rl_hbm, cl_hbm, pos_hbm, tg_hbm, gq_ref, gt_ref,
    q_ref, t_ref, rl_ref, cl_ref, pos_ref, tg_ref,
    qp, qo, ta, tb, cl1, cl2, cl3, own_sp, sp, xr, zs, zr, w, gts, g1, gr1, g2, gr2, load_sem, send_sem, recv_sem,
):
    rows, cols = q_ref.shape
    band = rows // (NX * NZ * NC)
    xband = band * NZ
    half = rows // 2
    b = lax.axis_index("dp")
    t = lax.axis_index("tensor")
    x, zl, c = t // (NZ * NC), lax.rem(t // NC, NZ), lax.rem(t, NC)

    pairs = ((q_hbm, q_ref), (t_hbm, t_ref), (cl_hbm, cl_ref), (rl_hbm, rl_ref), (pos_hbm, pos_ref), (tg_hbm, tg_ref))
    loads = [pltpu.make_async_copy(src, dst, load_sem.at[i]) for i, (src, dst) in enumerate(pairs)]
    for load in loads:
        load.start()

    def at_dp(k):
        return (lax.rem(b + k + n_dp, n_dp), t)

    def at_x(k):
        return (b, lax.rem(x + k, NX) * (NZ * NC) + zl * NC + c)

    def at_z(k):
        return (b, x * (NZ * NC) + lax.rem(zl + k, NZ) * NC + c)

    mate = (b, t + 1 - 2 * c)

    barrier = pltpu.get_barrier_semaphore()
    partners = [mate] + [at_x(k) for k in (1, 2, 3)] + [at_z(k) for k in (1, 2)]
    partners += [at_dp(k) for k in (1, -1, 2, -2, 3, -3)]
    for dev in partners:
        pl.semaphore_signal(barrier, inc=1, device_id=dev, device_id_type=pl.DeviceIdType.MESH)

    loads[0].wait()
    for i in range(NX * NZ):
        for p in range(NC):
            qp[p, band * i : band * (i + 1)] = q_ref[band * (NC * i + p) : band * (NC * i + p + 1)]
    loads[1].wait()
    loads[2].wait()

    pl.semaphore_wait(barrier, len(partners))

    started = []

    def send(src, dst, dev):
        i = len(started)
        copy = pltpu.make_async_remote_copy(
            src_ref=src, dst_ref=dst, send_sem=send_sem.at[i], recv_sem=recv_sem.at[i],
            device_id=dev, device_id_type=pl.DeviceIdType.MESH,
        )
        copy.start()
        started.append(copy)
        return copy

    cls = (cl1, cl2, cl3)
    own = [t_ref, ta.at[0], ta.at[1], ta.at[2]]
    got_q = send(qp.at[1 - c], qo, mate)
    low, high = pl.ds(0, half), pl.ds(half, half)
    got_tb = [[] for _ in range(STEPS)]
    got_tb[0].append(send(t_ref, tb.at[0], mate))
    got_t1 = [send(t_ref.at[low], ta.at[0, low], at_dp(1))]
    got_t3 = [send(t_ref.at[high], ta.at[2, high], at_dp(3))]
    got_t1.append(send(t_ref.at[high], ta.at[0, high], at_dp(1)))
    got_t3.append(send(t_ref.at[low], ta.at[2, low], at_dp(3)))
    got_cl = [None] + [send(cl_ref, cls[k - 1], at_dp(k)) for k in (1, 2, 3)]

    for load in loads[3:]:
        load.wait()
    lane = lax.broadcasted_iota(jnp.int32, (xband, rows), 1)
    row = lax.broadcasted_iota(jnp.int32, (xband, rows), 0)
    here = lane == ((x * NZ + row // band) * NC + c) * band + row % band
    rl = jnp.sum(jnp.where(here, rl_ref[...].reshape(1, rows), 0.0), axis=1, keepdims=True)
    pos = jnp.sum(jnp.where(here, pos_ref[...].reshape(1, rows), 0), axis=1, keepdims=True)

    reach = BOUND * BOUND * SCALE * cols * NC
    encode_x, decode_x = code_of(reach, 0.3)
    encode_z, decode_z = code_of(reach * NX, 0.6)

    got_x, got_z, got_xw, got_cw = {}, {}, {}, {}

    def scores(d):
        for copy in got_tb[d]:
            copy.wait_recv()
        qq = jnp.concatenate([qp[c], qo[...]], axis=1)
        tt = jnp.concatenate([own[d][...], tb[d]], axis=1)
        s = lax.dot_general(qq, tt, (((1,), (1,)), ((), ())), preferred_element_type=F32) * SCALE
        own_sp[d] = s.reshape(NX, xband, rows)
        sp[d] = encode_x(s).reshape(NX, xband, rows)
        got_x[d] = [send(sp.at[d, lax.rem(x + k, NX)], xr.at[d, k - 1], at_x(k)) for k in (1, 2, 3)]

    def sum_x(d):
        for copy in got_x[d]:
            copy.wait_recv()
        s = own_sp[d, x] + decode_x(xr[d, 0]) + decode_x(xr[d, 1]) + decode_x(xr[d, 2])
        own_sp[d, x] = s
        zs[d] = encode_z(s)
        got_z[d] = [send(zs.at[d], zr.at[d, k - 1], at_z(k)) for k in (1, 2)]

    def weigh(d):
        for copy in got_z[d]:
            copy.wait_recv()
        s = own_sp[d, x] + decode_z(zr[d, 0]) + decode_z(zr[d, 1])
        if d:
            got_cl[d].wait_recv()
        cl = (cls[d - 1] if d else cl_ref)[...].reshape(1, rows)
        match = (pos == lax.rem(b - d + n_dp, n_dp) * rows + lane).astype(F32)
        w[d, c, x] = (jnp.exp(s - rl) + jnp.exp(s - cl) - 2.0 * match).astype(BF16)
        got_xw[d] = [send(w.at[d, c, x], w.at[d, c, x], at_x(k)) for k in (1, 2, 3)]
        got_cw[d] = [send(w.at[d, c, x], w.at[d, c, x], mate)]

    def relay(d):
        for k in (1, 3, 2):
            got_xw[d][k - 1].wait_recv()
            piece = w.at[d, c, lax.rem(x + NX - k, NX)]
            got_cw[d].append(send(piece, piece, mate))

    def share(d, part):
        got_tb[d].append(send(ta.at[d - 1, part], tb.at[d, part], mate))

    def target_term(d):
        for copy in got_cw[d]:
            copy.wait_recv()
        weights = w[d].reshape(rows, rows)
        queries = qp[...].reshape(rows, cols)
        return lax.dot_general(weights, queries, (((0,), (0,)), ((), ())), preferred_element_type=F32) * SCALE

    got_q.wait_recv()
    scores(0)
    got_t1[0].wait_recv()
    got_t2a = send(ta.at[0, low], ta.at[1, low], at_dp(1))
    share(1, low)
    got_t3[0].wait_recv()
    got_t2b = send(ta.at[2, high], ta.at[1, high], at_dp(-1))
    share(3, high)
    sum_x(0)
    got_t1[1].wait_recv()
    share(1, high)
    got_t3[1].wait_recv()
    share(3, low)
    scores(1)
    scores(3)
    weigh(0)
    sum_x(1)
    got_t2a.wait_recv()
    share(2, low)
    got_t2b.wait_recv()
    share(2, high)
    relay(0)
    scores(2)
    weigh(1)
    sum_x(2)
    sum_x(3)
    relay(1)
    g1[...] = target_term(1).astype(BF16).reshape(g1.shape)
    got_1a = send(g1.at[0], gr1.at[0], at_dp(1))
    got_1b = send(g1.at[1], gr1.at[1], at_dp(-1))
    weigh(2)
    gts[0] = target_term(0) + tg_ref[...]
    g2[0, low] = gts[0, low].astype(BF16)
    got_g = [send(g2.at[0, low], gr2.at[0, low], at_dp(3))]
    weigh(3)
    relay(2)
    got_1b.wait_recv()
    g2[0, high] = (gts[0, high] + gr1[1].astype(F32)).astype(BF16)
    got_g.append(send(g2.at[0, high], gr2.at[0, high], at_dp(3)))
    gts[1] = target_term(2)
    g2[1, high] = gts[1, high].astype(BF16)
    got_g.append(send(g2.at[1, high], gr2.at[1, high], at_dp(1)))
    got_1a.wait_recv()
    g2[1, low] = (gts[1, low] + gr1[0].astype(F32)).astype(BF16)
    got_g.append(send(g2.at[1, low], gr2.at[1, low], at_dp(1)))
    relay(3)
    gts[0] = target_term(3)
    total = jnp.dot(w[0].reshape(rows, rows), t_ref[...], preferred_element_type=F32)
    for d in range(1, STEPS):
        total += jnp.dot(w[d].reshape(rows, rows), ta[d - 1], preferred_element_type=F32)
    for p in range(NC):
        for i in range(NX * NZ):
            piece = total[half * p + band * i : half * p + band * (i + 1)]
            gq_ref[band * (NC * i + p) : band * (NC * i + p + 1)] = piece * SCALE
    for copy in got_g:
        copy.wait_recv()
    gt_ref[...] = gts[0] + (gr2[0].astype(F32) + gr2[1].astype(F32))
    for copy in started:
        copy.wait_send()


def shards(n_dp, queries, targets, row_lse, col_lse, positive, target_grads):
    rows, cols = queries.shape
    band, half = rows // (NX * NZ * NC), rows // 2
    hbm = pl.BlockSpec(memory_space=pltpu.HBM)
    return pl.pallas_call(
        functools.partial(kernel, n_dp),
        out_shape=(pltpu.VMEM((rows, cols), F32),) * 2,
        in_specs=[hbm] * 6,
        out_specs=(pl.BlockSpec(memory_space=pltpu.VMEM),) * 2,
        scratch_shapes=[
            pltpu.VMEM((rows, cols), BF16),
            pltpu.VMEM((rows, cols), BF16),
            pltpu.VMEM((rows,), F32),
            pltpu.VMEM((rows,), F32),
            pltpu.VMEM((rows,), jnp.int32),
            pltpu.VMEM((rows, cols), F32),
            pltpu.VMEM((NC, half, cols), BF16),
            pltpu.VMEM((half, cols), BF16),
            pltpu.VMEM((STEPS - 1, rows, cols), BF16),
            pltpu.VMEM((STEPS, rows, cols), BF16),
            pltpu.VMEM((rows,), F32),
            pltpu.VMEM((rows,), F32),
            pltpu.VMEM((rows,), F32),
            pltpu.VMEM((STEPS, NX, band * NZ, rows), F32),
            pltpu.VMEM((STEPS, NX, band * NZ, rows), I16),
            pltpu.VMEM((STEPS, NX - 1, band * NZ, rows), I16),
            pltpu.VMEM((STEPS, band * NZ, rows), I16),
            pltpu.VMEM((STEPS, NZ - 1, band * NZ, rows), I16),
            pltpu.VMEM((STEPS, NC, NX, band * NZ, rows), BF16),
            pltpu.VMEM((2, rows, cols), F32),
            pltpu.VMEM((2, half, cols), BF16),
            pltpu.VMEM((2, half, cols), BF16),
            pltpu.VMEM((2, rows, cols), BF16),
            pltpu.VMEM((2, rows, cols), BF16),
            pltpu.SemaphoreType.DMA((LOADS,)),
            pltpu.SemaphoreType.DMA((COPIES,)),
            pltpu.SemaphoreType.DMA((COPIES,)),
        ],
        compiler_params=pltpu.CompilerParams(
            collective_id=0, has_side_effects=True, vmem_limit_bytes=56 << 20
        ),
        cost_estimate=pl.CostEstimate(flops=10**9, bytes_accessed=10**6, transcendentals=10**5),
    )(
        queries, targets, row_lse, col_lse, positive, target_grads
    )


def solution(mesh):
    placed = (P("dp", "tensor"), P("dp", "tensor"), P("dp"), P("dp"), P("dp"), P("dp", "tensor"))
    return jax.shard_map(
        functools.partial(shards, mesh.shape["dp"]),
        mesh=mesh,
        in_specs=placed,
        out_specs=(P("dp", "tensor"), P("dp", "tensor")),
        check_vma=False,
    )
```

time: 78.3 us -> 65.7 us (0.84); the launches traced: 77.1 us -> 65.5 us
  Pallas kernels: 71 us -> 63.5 us
  local copies, waits for them, and re-layouts: 5.44 us -> 1.36 us
    pallas_call x1, Pallas kernels: 71 us -> 63.5 us  [shards(): pl.pallas_call(functools.partial(kernel, n_dp), out_shape=(pltpu.VMEM((ro...]
    unnamed x12 -> x2, local copies, waits for them, and re-layouts: 4.75 us -> 1.36 us
where the time goes in v2:
time: 65.7 us; the launch traced here: 65.5 us
  Pallas kernels  63.5 us (97%)
  local copies, waits for them, and re-layouts  1.36 us (2%)
    pallas_call x1, Pallas kernels, shards(): pl.pallas_call(functools.partial(kernel, n_dp), out_shape=(pltpu.VMEM((ro...  63.5 us
    unnamed x2, local copies, waits for them, and re-layouts  1.36 us

profile of v2, /device:TPU:1, one launch (start us, length us, event | category | flops | bytes accessed | tf_op | source)
XLA Modules:
  0.0 65.5 jit_solution(5365598071577469692)
XLA Ops:
  0.6 63.5 %shard_map.77 = (f32[384,128]{1,0:T(8,128)S(1)}, f32[384,128]{1,0:T(8,128)S(1)}) custom-call(bf16[384,128]{1,0:T(8,128)(2,1)} %q_hbm.1, bf16[384,128]{1,0:T(8,128)(2,1)} %t_hbm.1, f32[384]{0:T(512)} %rl_hbm.1, f32[384]{0:T(512)} %cl_hbm.1, s32[384]{0:T(512)} %pos_hbm.1, f32[384,128]{1,0:T(8,128)} %tg_hbm.1), custom_call_target="tpu_custom_call" | custom-call | flops 1000000000 | bytes 1000000 | tf_op jit(solution)/shard_map/pallas_call | solution.py:232
  64.2 0.7 %copy.10 = f32[384,128]{1,0:T(8,128)} copy(f32[384,128]{1,0:T(8,128)S(1)} %get-tuple-element.2) | data formatting | bytes 393216
  64.9 0.7 %copy.11 = f32[384,128]{1,0:T(8,128)} copy(f32[384,128]{1,0:T(8,128)S(1)} %get-tuple-element.3) | data formatting | bytes 393216

commit v3 on v1

--- a/solution.py
+++ b/solution.py
@@ -12,16 +12,18 @@
 STEPS = 4
 NX, NZ, NC = 4, 3, 2
 SCALE = 2.0 / math.sqrt(D)
-COPIES = 64
+COPIES = 80
+LOADS = 6
 F32 = jnp.float32
 BF16 = jnp.bfloat16
 
 
 def kernel(
-    n_dp, q_ref, t_ref, rl_ref, cl_ref, pos_ref, tg_ref, gq_ref, gt_ref,
-    qp, qo, ta, tb, cls, sp, xr, zs, zr, w, gts, g1, gr1, g2, gr2, send_sem, recv_sem,
+    n_dp, q_hbm, t_hbm, rl_hbm, cl_hbm, pos_hbm, tg_hbm, gq_ref, gt_ref,
+    q_ref, t_ref, rl_ref, cl_ref, pos_ref, tg_ref,
+    qp, qo, ta, tb, cl1, cl2, cl3, sp, xr, zs, zr, w, gts, g1, gr1, g2, gr2, load_sem, send_sem, recv_sem,
 ):
-    rows = q_ref.shape[0]
+    rows, cols = q_ref.shape
     band = rows // (NX * NZ * NC)
     xband = band * NZ
     half = rows // 2
@@ -29,6 +31,11 @@
     t = lax.axis_index("tensor")
     x, zl, c = t // (NZ * NC), lax.rem(t // NC, NZ), lax.rem(t, NC)
 
+    pairs = ((q_hbm, q_ref), (t_hbm, t_ref), (cl_hbm, cl_ref), (rl_hbm, rl_ref), (pos_hbm, pos_ref), (tg_hbm, tg_ref))
+    loads = [pltpu.make_async_copy(src, dst, load_sem.at[i]) for i, (src, dst) in enumerate(pairs)]
+    for load in loads:
+        load.start()
+
     def at_dp(k):
         return (lax.rem(b + k + n_dp, n_dp), t)
 
@@ -46,9 +53,12 @@
     for dev in partners:
         pl.semaphore_signal(barrier, inc=1, device_id=dev, device_id_type=pl.DeviceIdType.MESH)
 
+    loads[0].wait()
     for i in range(NX * NZ):
         for p in range(NC):
             qp[p, band * i : band * (i + 1)] = q_ref[band * (NC * i + p) : band * (NC * i + p + 1)]
+    loads[1].wait()
+    loads[2].wait()
 
     pl.semaphore_wait(barrier, len(partners))
 
@@ -64,18 +74,21 @@
         started.append(copy)
         return copy
 
+    cls = (cl1, cl2, cl3)
     own = [t_ref, ta.at[0], ta.at[1], ta.at[2]]
     got_q = send(qp.at[1 - c], qo, mate)
     got_tb = [None] * STEPS
     got_tb[0] = send(t_ref, tb.at[0], mate)
     got_t1 = send(t_ref, ta.at[0], at_dp(1))
     got_t3 = send(t_ref, ta.at[2], at_dp(3))
-    got_cl = [None] + [send(cl_ref, cls.at[k - 1], at_dp(k)) for k in (1, 2, 3)]
-
+    got_cl = [None] + [send(cl_ref, cls[k - 1], at_dp(k)) for k in (1, 2, 3)]
+
+    for load in loads[3:]:
+        load.wait()
     lane = lax.broadcasted_iota(jnp.int32, (band, rows), 1)
     here = lane == t * band + lax.broadcasted_iota(jnp.int32, (band, rows), 0)
-    rl = jnp.sum(jnp.where(here, rl_ref[...], 0.0), axis=1, keepdims=True)
-    pos = jnp.sum(jnp.where(here, pos_ref[...], 0), axis=1, keepdims=True)
+    rl = jnp.sum(jnp.where(here, rl_ref[...].reshape(1, rows), 0.0), axis=1, keepdims=True)
+    pos = jnp.sum(jnp.where(here, pos_ref[...].reshape(1, rows), 0), axis=1, keepdims=True)
 
     got_x, got_z, got_zw, got_xw, got_cw = {}, {}, {}, {}, {}
 
@@ -100,38 +113,39 @@
         s = (zs[d, zl] + zr[d, 0] + zr[d, 1]) * SCALE
         if d:
             got_cl[d].wait_recv()
-        cl = cls[d - 1] if d else cl_ref[...]
+        cl = (cls[d - 1] if d else cl_ref)[...].reshape(1, rows)
         match = (pos == lax.rem(b - d + n_dp, n_dp) * rows + lane).astype(F32)
-        band_w = jnp.exp(s - rl) + jnp.exp(s - cl) - 2.0 * match
         mine = pl.ds(pl.multiple_of(zl * band, band), band)
-        w[d, c, x, mine] = band_w.astype(BF16)
+        w[d, c, x, mine] = (jnp.exp(s - rl) + jnp.exp(s - cl) - 2.0 * match).astype(BF16)
         got_zw[d] = [send(w.at[d, c, x, mine], w.at[d, c, x, mine], at_z(k)) for k in (1, 2)]
 
     def gather_x(d):
-        for k, copy in enumerate(got_zw[d]):
+        for copy in got_zw[d]:
             copy.wait_recv()
         got_xw[d] = [send(w.at[d, c, x], w.at[d, c, x], at_x(k)) for k in (1, 2, 3)]
-
-    def gather_core(d):
-        for copy in got_xw[d]:
-            copy.wait_recv()
-        got_cw[d] = send(w.at[d, c], w.at[d, c], mate)
-
-    def gradients(d):
-        got_cw[d].wait_recv()
+        got_cw[d] = [send(w.at[d, c, x], w.at[d, c, x], mate)]
+
+    def relay(d):
+        for k in (1, 3, 2):
+            got_xw[d][k - 1].wait_recv()
+            piece = w.at[d, c, lax.rem(x + NX - k, NX)]
+            got_cw[d].append(send(piece, piece, mate))
+
+    def gradients(d, first=False):
+        for copy in got_cw[d]:
+            copy.wait_recv()
         weights = w[d].reshape(rows, rows)
         part = jnp.dot(weights, own[d][...], preferred_element_type=F32) * SCALE
         for p in range(NC):
             for i in range(NX * NZ):
                 to = slice(band * (NC * i + p), band * (NC * i + p + 1))
                 piece = part[half * p + band * i : half * p + band * (i + 1)]
-                gq_ref[to] = piece if d == 1 else gq_ref[to] + piece
-        queries = qp[...].reshape(rows, q_ref.shape[1])
+                gq_ref[to] = piece if first else gq_ref[to] + piece
+        queries = qp[...].reshape(rows, cols)
         term = lax.dot_general(weights, queries, (((0,), (0,)), ((), ())), preferred_element_type=F32)
         return term * SCALE
 
-    scores_0_ready = got_q
-    scores_0_ready.wait_recv()
+    got_q.wait_recv()
     scores(0)
     sum_x(0)
     got_t1.wait_recv()
@@ -141,36 +155,36 @@
     got_t2b = send(ta.at[2, pl.ds(half, half)], ta.at[1, pl.ds(half, half)], at_dp(-1))
     got_tb[3] = send(ta.at[2], tb.at[3], mate)
     scores(1)
+    weigh(0)
     scores(3)
-    weigh(0)
     sum_x(1)
+    gather_x(0)
     sum_x(3)
-    gather_x(0)
-    weigh(1)
-    weigh(3)
     got_t2a.wait_recv()
     got_t2b.wait_recv()
     got_tb[2] = send(ta.at[1], tb.at[2], mate)
+    weigh(1)
+    scores(2)
+    relay(0)
+    weigh(3)
     gather_x(1)
+    sum_x(2)
     gather_x(3)
-    scores(2)
-    gather_core(0)
-    sum_x(2)
-    gather_core(1)
-    gather_core(3)
-    weigh(2)
-    term = gradients(1)
+    relay(1)
+    term = gradients(1, first=True)
     g1[...] = term.astype(BF16).reshape(g1.shape)
     got_1a = send(g1.at[0], gr1.at[0], at_dp(1))
     got_1b = send(g1.at[1], gr1.at[1], at_dp(-1))
+    weigh(2)
+    gts[0] = gradients(0) + tg_ref[...]
+    relay(3)
     gather_x(2)
-    gts[0] = gradients(0) + tg_ref[...]
+    gts[1] = gradients(3)
+    relay(2)
     got_1b.wait_recv()
     g2[0, :half] = gts[0, :half].astype(BF16)
     g2[0, half:] = (gts[0, half:] + gr1[1].astype(F32)).astype(BF16)
     got_20 = send(g2.at[0], gr2.at[0], at_dp(3))
-    gts[1] = gradients(3)
-    gather_core(2)
     gts[0] = gradients(2)
     got_1a.wait_recv()
     g2[1, :half] = (gts[0, :half] + gr1[0].astype(F32)).astype(BF16)
@@ -186,18 +200,26 @@
 def shards(n_dp, queries, targets, row_lse, col_lse, positive, target_grads):
     rows, cols = queries.shape
     band, half = rows // (NX * NZ * NC), rows // 2
-    vmem = pl.BlockSpec(memory_space=pltpu.VMEM)
+    hbm = pl.BlockSpec(memory_space=pltpu.HBM)
     return pl.pallas_call(
         functools.partial(kernel, n_dp),
-        out_shape=(jax.ShapeDtypeStruct((rows, cols), F32),) * 2,
-        in_specs=[vmem] * 6,
-        out_specs=(vmem, vmem),
+        out_shape=(pltpu.VMEM((rows, cols), F32),) * 2,
+        in_specs=[hbm] * 6,
+        out_specs=(pl.BlockSpec(memory_space=pltpu.VMEM),) * 2,
         scratch_shapes=[
+            pltpu.VMEM((rows, cols), BF16),
+            pltpu.VMEM((rows, cols), BF16),
+            pltpu.VMEM((rows,), F32),
+            pltpu.VMEM((rows,), F32),
+            pltpu.VMEM((rows,), jnp.int32),
+            pltpu.VMEM((rows, cols), F32),
             pltpu.VMEM((NC, half, cols), BF16),
             pltpu.VMEM((half, cols), BF16),
             pltpu.VMEM((STEPS - 1, rows, cols), BF16),
             pltpu.VMEM((STEPS, rows, cols), BF16),
-            pltpu.VMEM((STEPS - 1, 1, rows), F32),
+            pltpu.VMEM((rows,), F32),
+            pltpu.VMEM((rows,), F32),
+            pltpu.VMEM((rows,), F32),
             pltpu.VMEM((STEPS, NX, band * NZ, rows), F32),
             pltpu.VMEM((STEPS, NX - 1, band * NZ, rows), F32),
             pltpu.VMEM((STEPS, NZ, band, rows), F32),
@@ -208,16 +230,16 @@
             pltpu.VMEM((2, half, cols), BF16),
             pltpu.VMEM((2, rows, cols), BF16),
             pltpu.VMEM((2, rows, cols), BF16),
+            pltpu.SemaphoreType.DMA((LOADS,)),
             pltpu.SemaphoreType.DMA((COPIES,)),
             pltpu.SemaphoreType.DMA((COPIES,)),
         ],
         compiler_params=pltpu.CompilerParams(
-            collective_id=0, has_side_effects=True, vmem_limit_bytes=40 << 20
+            collective_id=0, has_side_effects=True, vmem_limit_bytes=56 << 20
         ),
         cost_estimate=pl.CostEstimate(flops=10**9, bytes_accessed=10**6, transcendentals=10**5),
     )(
-        queries, targets, row_lse.reshape(1, rows), col_lse.reshape(1, rows),
-        positive.reshape(1, rows), target_grads,
+        queries, targets, row_lse, col_lse, positive, target_grads
     )
 
 

time: 78.3 us -> 70.1 us (0.90)
  local copies, waits for them, and re-layouts: 5.44 us -> 1.36 us
  Pallas kernels: 71 us -> 67.3 us
    pallas_call x1, Pallas kernels: 71 us -> 67.3 us  [shards(): pl.pallas_call(functools.partial(kernel, n_dp), out_shape=(pltpu.VMEM((ro...]
    unnamed x12 -> x2, local copies, waits for them, and re-layouts: 4.75 us -> 1.36 us
where the time goes in v3:
time: 70.1 us; the launch traced here: 69.3 us
  Pallas kernels  67.3 us (96%)
  local copies, waits for them, and re-layouts  1.36 us (2%)
    pallas_call x1, Pallas kernels, shards(): pl.pallas_call(functools.partial(kernel, n_dp), out_shape=(pltpu.VMEM((ro...  67.3 us

profile of v3, /device:TPU:1, one launch (start us, length us, event | category | flops | bytes accessed | tf_op | source)
XLA Modules:
  0.0 69.3 jit_solution(2673610491401345201)
XLA Ops:
  0.6 67.3 %shard_map.77 = (f32[384,128]{1,0:T(8,128)S(1)}, f32[384,128]{1,0:T(8,128)S(1)}) custom-call(bf16[384,128]{1,0:T(8,128)(2,1)} %q_hbm.1, bf16[384,128]{1,0:T(8,128)(2,1)} %t_hbm.1, f32[384]{0:T(512)} %rl_hbm.1, f32[384]{0:T(512)} %cl_hbm.1, s32[384]{0:T(512)} %pos_hbm.1, f32[384,128]{1,0:T(8,128)} %tg_hbm.1), custom_call_target="tpu_custom_call" | custom-call | flops 1000000000 | bytes 1000000 | tf_op jit(solution)/shard_map/pallas_call | solution.py:204
  68.0 0.7 copy.10
  68.7 0.7 copy.11

commit v4 on v3

--- a/solution.py
+++ b/solution.py
@@ -159,23 +159,23 @@
     scores(3)
     sum_x(1)
     gather_x(0)
-    sum_x(3)
     got_t2a.wait_recv()
     got_t2b.wait_recv()
     got_tb[2] = send(ta.at[1], tb.at[2], mate)
+    sum_x(3)
     weigh(1)
     scores(2)
     relay(0)
+    gather_x(1)
     weigh(3)
-    gather_x(1)
     sum_x(2)
     gather_x(3)
     relay(1)
+    weigh(2)
     term = gradients(1, first=True)
     g1[...] = term.astype(BF16).reshape(g1.shape)
     got_1a = send(g1.at[0], gr1.at[0], at_dp(1))
     got_1b = send(g1.at[1], gr1.at[1], at_dp(-1))
-    weigh(2)
     gts[0] = gradients(0) + tg_ref[...]
     relay(3)
     gather_x(2)

time: 70.1 us -> 67.7 us (0.966)
  Pallas kernels: 67.3 us -> 65.1 us
    pallas_call x1, Pallas kernels: 67.3 us -> 65.1 us  [shards(): pl.pallas_call(functools.partial(kernel, n_dp), out_shape=(pltpu.VMEM((ro...]
where the time goes in v4:
time: 67.7 us; the launch traced here: 67.1 us
  Pallas kernels  65.1 us (96%)
  local copies, waits for them, and re-layouts  1.36 us (2%)
    pallas_call x1, Pallas kernels, shards(): pl.pallas_call(functools.partial(kernel, n_dp), out_shape=(pltpu.VMEM((ro...  65.1 us
    unnamed x2, local copies, waits for them, and re-layouts  1.36 us

profile of v4, /device:TPU:1, one launch (start us, length us, event | category | flops | bytes accessed | tf_op | source)
XLA Modules:
  0.0 67.1 jit_solution(14426686941443074551)
XLA Ops:
  0.6 65.1 %shard_map.77 = (f32[384,128]{1,0:T(8,128)S(1)}, f32[384,128]{1,0:T(8,128)S(1)}) custom-call(bf16[384,128]{1,0:T(8,128)(2,1)} %q_hbm.1, bf16[384,128]{1,0:T(8,128)(2,1)} %t_hbm.1, f32[384]{0:T(512)} %rl_hbm.1, f32[384]{0:T(512)} %cl_hbm.1, s32[384]{0:T(512)} %pos_hbm.1, f32[384,128]{1,0:T(8,128)} %tg_hbm.1), custom_call_target="tpu_custom_call" | custom-call | flops 1000000000 | bytes 1000000 | tf_op jit(solution)/shard_map/pallas_call | solution.py:204
  65.7 0.7 %copy.10 = f32[384,128]{1,0:T(8,128)} copy(f32[384,128]{1,0:T(8,128)S(1)} %get-tuple-element.2) | data formatting | bytes 393216
  66.4 0.7 %copy.11 = f32[384,128]{1,0:T(8,128)} copy(f32[384,128]{1,0:T(8,128)S(1)} %get-tuple-element.3) | data formatting | bytes 393216

commit v5 on v4

--- a/solution.py
+++ b/solution.py
@@ -163,8 +163,8 @@
     got_t2b.wait_recv()
     got_tb[2] = send(ta.at[1], tb.at[2], mate)
     sum_x(3)
+    scores(2)
     weigh(1)
-    scores(2)
     relay(0)
     gather_x(1)
     weigh(3)
@@ -176,10 +176,9 @@
     g1[...] = term.astype(BF16).reshape(g1.shape)
     got_1a = send(g1.at[0], gr1.at[0], at_dp(1))
     got_1b = send(g1.at[1], gr1.at[1], at_dp(-1))
-    gts[0] = gradients(0) + tg_ref[...]
     relay(3)
     gather_x(2)
-    gts[1] = gradients(3)
+    gts[0] = gradients(0) + tg_ref[...]
     relay(2)
     got_1b.wait_recv()
     g2[0, :half] = gts[0, :half].astype(BF16)
@@ -190,6 +189,7 @@
     g2[1, :half] = (gts[0, :half] + gr1[0].astype(F32)).astype(BF16)
     g2[1, half:] = gts[0, half:].astype(BF16)
     got_22 = send(g2.at[1], gr2.at[1], at_dp(1))
+    gts[1] = gradients(3)
     got_20.wait_recv()
     got_22.wait_recv()
     gt_ref[...] = gts[1] + (gr2[0].astype(F32) + gr2[1].astype(F32))

time: 67.7 us -> 68 us (level)
  the two profiles are of different devices: /device:TPU:1 before, /device:TPU:128 now
where the time goes in v5:
time: 68 us; the launch traced here: 67.9 us
  Pallas kernels  65.9 us (97%)
  local copies, waits for them, and re-layouts  1.36 us (2%)
    pallas_call x1, Pallas kernels, shards(): pl.pallas_call(functools.partial(kernel, n_dp), out_shape=(pltpu.VMEM((ro...  65.9 us

profile of v5, /device:TPU:128, one launch (start us, length us, event | category | flops | bytes accessed | tf_op | source)
XLA Modules:
  0.0 67.9 jit_solution(1519974015019485194)
XLA Ops:
  0.6 65.9 %shard_map.77 = (f32[384,128]{1,0:T(8,128)S(1)}, f32[384,128]{1,0:T(8,128)S(1)}) custom-call(bf16[384,128]{1,0:T(8,128)(2,1)} %q_hbm.1, bf16[384,128]{1,0:T(8,128)(2,1)} %t_hbm.1, f32[384]{0:T(512)} %rl_hbm.1, f32[384]{0:T(512)} %cl_hbm.1, s32[384]{0:T(512)} %pos_hbm.1, f32[384,128]{1,0:T(8,128)} %tg_hbm.1), custom_call_target="tpu_custom_call" | custom-call | flops 1000000000 | bytes 1000000 | tf_op jit(solution)/shard_map/pallas_call | solution.py:204
  66.5 0.7 %copy.10 = f32[384,128]{1,0:T(8,128)} copy(f32[384,128]{1,0:T(8,128)S(1)} %get-tuple-element.2) | data formatting | bytes 393216
  67.2 0.7 copy.11
